TPU v7x, 32 devices: a whole 2x2x4 slice. The times are simulated.
32 devices in a mesh: dp: 8 (over z, core), expert: 4 (over y, x).
Axes of the slice: x: 2, y: 2, z: 4, core: 2. Of those that a mesh axis runs over, the one named last changes fastest.
Arguments:
- tokens: bfloat16 [4, 1024, 3584], P('expert', 'dp'), may hold values from -6 to 6
- grad_out: bfloat16 [4, 1024, 3584], P('expert', 'dp'), may hold values from -6 to 6
- route_ids: int32 [4, 1024], P('expert', 'dp'), may hold values from 0 to 3, as said below
- route_gates: float32 [4, 1024], P('expert', 'dp'), may hold values from 0.2 to 1
- w_gate: bfloat16 [4, 3584, 1024], P('expert', 'dp'), may hold values from -0.09375 to 0.09375
- w_up: bfloat16 [4, 3584, 1024], P('expert', 'dp'), may hold values from -0.09375 to 0.09375
- w_down: bfloat16 [4, 1024, 3584], P('expert', 'dp'), may hold values from -0.1875 to 0.1875
Outputs:
- moe_out: bfloat16 [4, 1024, 3584], P('expert', 'dp')
- input_grad: bfloat16 [4, 1024, 3584], P('expert', None, 'dp')
- gate_grad: float32 [4, 1024], P('expert', 'dp')
Inputs may be any that keep to these rules, and one draw needn't show every extreme that they name: `route_ids`: among the 128 tokens of one device at most 80 name the same expert; one expert is named by exactly 80 tokens of every device; on one device the counts of the other experts differ by at most one.
All inputs are finite; a program needn't handle non-finite values.
Results may differ from a plain program's by a relative error of at most 0.0057.
Values may be sent and summed in bfloat16 or wider, within the bound.
A program may use at most 128 MiB of HBM per device.

v0:
```python
import jax
import jax.numpy as jnp
from jax import lax
from jax.sharding import PartitionSpec as P

F32 = jnp.float32
BF16 = jnp.bfloat16
DOWN_PARTS = 2


def placement(route_line, expert_count, capacity):
    tok_count = route_line.shape[0]
    same = route_line[:, None] == route_line[None, :]
    earlier = jnp.arange(tok_count)[None, :] < jnp.arange(tok_count)[:, None]
    placed = jnp.sum((same & earlier).astype(jnp.int32), axis=1)
    slots = route_line * capacity + placed
    rows = jnp.arange(expert_count * capacity, dtype=jnp.int32)
    return (rows[:, None] == slots[None, :]).astype(BF16)


def mm(a, b, dims=(((1,), (0,)), ((), ()))):
    return lax.dot_general(a, b, dims, preferred_element_type=F32)


NT = (((1,), (1,)), ((), ()))
TN = (((0,), (0,)), ((), ()))


def local(tokens, grad_out, route_ids, route_gates, w_gate, w_up, w_down):
    expert_count = lax.axis_size("expert")
    dp_count = lax.axis_size("dp")
    tok_count = tokens.shape[1]
    width = tokens.shape[2]
    capacity = max(2, 5 * tok_count // (2 * expert_count))
    place = placement(route_ids[0], expert_count, capacity)
    own_grad = grad_out[0].astype(F32)
    gate_column = route_gates[0][:, None]
    scaled_grad = (gate_column * own_grad).astype(BF16)

    def over_experts(rows):
        cols = rows.shape[1]
        got = lax.all_to_all(
            rows.reshape(expert_count, capacity, cols),
            "expert",
            split_axis=0,
            concat_axis=0,
            tiled=True,
        )
        return got.reshape(expert_count * capacity, cols)

    gate_matrix = lax.all_gather(w_gate, "dp", axis=1, tiled=True)[0]
    up_matrix = lax.all_gather(w_up, "dp", axis=1, tiled=True)[0]
    w_down, _ = lax.optimization_barrier((w_down, gate_matrix[:16, :128]))
    step = width // DOWN_PARTS
    spans = [slice(i * step, (i + 1) * step) for i in range(DOWN_PARTS)]
    downs = [lax.all_gather(w_down[:, :, s], "dp", axis=1, tiled=True)[0] for s in spans]
    routed = over_experts(mm(place, tokens[0]).astype(BF16))
    routed_grad = over_experts(mm(place, scaled_grad).astype(BF16))
    gate_pre = mm(routed, gate_matrix)
    up_pre = mm(routed, up_matrix)
    sigmoid_gate = jax.nn.sigmoid(gate_pre)
    silu_gate = gate_pre * sigmoid_gate
    hidden = (silu_gate * up_pre).astype(BF16)
    moe_parts = []
    gate_grad = jnp.zeros((tok_count,), F32)
    hidden_grad = jnp.zeros_like(gate_pre)
    for s, down in zip(spans, downs):
        expert_out = mm(hidden, down).astype(BF16)
        hidden_grad = hidden_grad + mm(routed_grad[:, s], down, NT)
        token_out = mm(place, over_experts(expert_out), TN)
        moe_parts.append((gate_column * token_out).astype(BF16))
        gate_grad = gate_grad + jnp.sum(own_grad[:, s] * token_out, axis=1)
    moe_out = jnp.concatenate(moe_parts, axis=1)
    gate_pre_grad = (
        hidden_grad * up_pre * sigmoid_gate * (1.0 + gate_pre * (1.0 - sigmoid_gate))
    ).astype(BF16)
    up_pre_grad = (hidden_grad * silu_gate).astype(BF16)
    input_rows = (mm(gate_pre_grad, gate_matrix, NT) + mm(up_pre_grad, up_matrix, NT)).astype(BF16)
    home_rows = over_experts(input_rows)
    token_grad = mm(home_rows, place, TN).astype(BF16)
    parts = token_grad.reshape(dp_count, width // dp_count, tok_count)
    heads = lax.all_to_all(parts, "dp", split_axis=0, concat_axis=0, tiled=True)
    input_grad = heads.transpose(0, 2, 1).reshape(1, dp_count * tok_count, width // dp_count)
    return (moe_out[None], input_grad, gate_grad[None])


def solution(mesh):
    in_specs = (
        P("expert", "dp", None),
        P("expert", "dp", None),
        P("expert", "dp"),
        P("expert", "dp"),
        P("expert", "dp", None),
        P("expert", "dp", None),
        P("expert", "dp", None),
    )
    out_specs = (P("expert", "dp", None), P("expert", None, "dp"), P("expert", "dp"))
    return jax.shard_map(local, mesh=mesh, in_specs=in_specs, out_specs=out_specs, check_vma=False)
```

profile of v0, /device:TPU:0, one launch (start us, length us, event | category | flops | bytes accessed | tf_op | source)
XLA Modules:
  0.0 360.8 jit_solution(10377897107065206636)
XLA Ops:
  7.2 2.2 fusion.51
  11.7 2.3 convolution_convert_fusion
  14.0 5.2 %all-to-all-start.3 = ((bf16[4,80,3584]{2,1,0:T(8,128)(2,1)}), bf16[4,80,3584]{2,1,0:T(8,128)(2,1)S(1)}, u32[]{:S(2)}, u32[]{:S(2)}) async-start(bf16[4,80,3584]{2,1,0:T(8,128)(2,1)} %bitcast.17), calls=%async_computation.3 | async-start | bytes 4587520 | tf_op jit(solution)/shard_map/all_to_all | solution.py:42
  19.2 2.1 convolution_convert_fusion.1
  21.3 24.9 %all-to-all-done.3 = bf16[4,80,3584]{2,1,0:T(8,128)(2,1)S(1)} async-done(((bf16[4,80,3584]{2,1,0:T(8,128)(2,1)}), bf16[4,80,3584]{2,1,0:T(8,128)(2,1)S(1)}, u32[]{:S(2)}, u32[]{:S(2)}) %all-to-all-start.3) | async-done | bytes 2293792 | tf_op jit(solution)/shard_map/all_to_all | solution.py:42
  46.2 1.4 copy-done.5
  47.6 3.6 %all-to-all-start = ((bf16[4,80,3584]{2,1,0:T(8,128)(2,1)}), bf16[4,80,3584]{2,1,0:T(8,128)(2,1)S(1)}, u32[]{:S(2)}, u32[]{:S(2)}) async-start(bf16[4,80,3584]{2,1,0:T(8,128)(2,1)} %bitcast.5), calls=%async_computation | async-start | bytes 4587520 | tf_op jit(solution)/shard_map/all_to_all | solution.py:42
  51.3 4.3 %all-gather.11.cloned.1.call-done = bf16[1,1024,1792]{2,1,0:T(8,128)(2,1)} async-done(((bf16[1,128,1792]{2,1,0:T(8,128)(2,1)}), bf16[1,1024,1792]{2,1,0:T(8,128)(2,1)}) %all-gather.11.cloned.1.call-update) | async-done | bytes 3670032 | tf_op jit(solution)/shard_map/all_gather | solution.py:56
  55.6 4.8 %fusion.14 = f32[320,1024]{1,0:T(8,128)} fusion(bf16[1,1024,1792]{2,1,0:T(8,128)(2,1)} %all-gather.11.cloned.1.call-done, bf16[320,3584]{1,0:T(8,128)(2,1)} %bitcast.80), kind=kOutput, calls=%fused_computation.13 | convolution fusion | flops 1174405120 | bytes 6127616 | tf_op jit(solution)/shard_map/dot_general | solution.py:22
  60.4 38.9 %all-gather.9.cloned.1.call-done = bf16[1,1024,1792]{2,1,0:T(8,128)(2,1)} async-done(((bf16[1,128,1792]{2,1,0:T(8,128)(2,1)}), bf16[1,1024,1792]{2,1,0:T(8,128)(2,1)}) %all-gather.9.cloned.1.call-update) | async-done | bytes 3670032 | tf_op jit(solution)/shard_map/all_gather | solution.py:56
  99.3 5.2 %fusion.28 = f32[320,1024]{1,0:T(8,128)} fusion(f32[320,1024]{1,0:T(8,128)} %fusion.14, bf16[1,1024,1792]{2,1,0:T(8,128)(2,1)} %all-gather.9.cloned.1.call-done, bf16[320,3584]{1,0:T(8,128)(2,1)} %bitcast.81), kind=kOutput, calls=%fused_computation.24 | convolution fusion | flops 1174732800 | bytes 7438336 | tf_op jit(solution)/shard_map/dot_general | solution.py:22
  104.5 68.7 %all-gather.5.cloned.1.call-done = bf16[1,3584,1024]{2,1,0:T(8,128)(2,1)} async-done(((bf16[1,448,1024]{2,1,0:T(8,128)(2,1)}), bf16[1,3584,1024]{2,1,0:T(8,128)(2,1)}) %all-gather.5.cloned.1.call-update) | async-done | bytes 7340048 | tf_op jit(solution)/shard_map/all_gather | solution.py:51
  173.2 6.7 %fusion.6 = f32[320,1024]{1,0:T(8,128)} fusion(bf16[320,3584]{1,0:T(8,128)(2,1)S(1)} %bitcast.78, bf16[1,3584,1024]{2,1,0:T(8,128)(2,1)} %all-gather.5.cloned.1.call-done), kind=kOutput, calls=%fused_computation.6 | convolution fusion | flops 2348810240 | bytes 10944512 | tf_op jit(solution)/shard_map/dot_general | solution.py:22
  179.9 66.9 %all-gather.7.cloned.1.call-done = bf16[1,3584,1024]{2,1,0:T(8,128)(2,1)} async-done(((bf16[1,448,1024]{2,1,0:T(8,128)(2,1)}), bf16[1,3584,1024]{2,1,0:T(8,128)(2,1)}) %all-gather.7.cloned.1.call-update) | async-done | bytes 7340048 | tf_op jit(solution)/shard_map/all_gather | solution.py:52
  246.8 7.2 %multiply_convert_fusion.3 = (bf16[320,1024]{1,0:T(8,128)(2,1)S(1)}, f32[320,1024]{1,0:T(8,128)}) fusion(f32[320,1024]{1,0:T(8,128)} %fusion.6, bf16[320,3584]{1,0:T(8,128)(2,1)S(1)} %bitcast.79, bf16[1,3584,1024]{2,1,0:T(8,128)(2,1)} %all-gather.7.cloned.1.call-done), kind=kOutput, calls=%fused_computation.27 | convolution fusion | flops 2350776320 | bytes 12910592 | tf_op jit(solution)/shard_map/dot_general | solution.py:22
  254.1 2.5 fusion.22
  256.5 3.7 %all-to-all-start.1 = ((bf16[4,80,1792]{2,1,0:T(8,128)(2,1)}), bf16[4,80,1792]{2,1,0:T(8,128)(2,1)S(1)}, u32[]{:S(2)}, u32[]{:S(2)}) async-start(bf16[4,80,1792]{2,1,0:T(8,128)(2,1)} %bitcast.10), calls=%async_computation.1 | async-start | bytes 2293760 | tf_op jit(solution)/shard_map/all_to_all | solution.py:42
  260.3 6.6 %fusion = f32[320,3584]{1,0:T(8,128)S(1)} fusion(bf16[1,3584,1024]{2,1,0:T(8,128)(2,1)} %all-gather.7.cloned.1.call-done, f32[320,1024]{1,0:T(8,128)} %fusion.28, f32[320,1024]{1,0:T(8,128)} %fusion.6), kind=kOutput, calls=%fused_computation | convolution fusion | flops 2350776320 | bytes 14548992 | tf_op jit(solution)/shard_map/dot_general | solution.py:22
  266.9 7.4 %fusion.11 = bf16[320,3584]{1,0:T(8,128)(2,1)} fusion(f32[320,3584]{1,0:T(8,128)S(1)} %fusion, bf16[1,3584,1024]{2,1,0:T(8,128)(2,1)} %all-gather.5.cloned.1.call-done, f32[320,1024]{1,0:T(8,128)S(1)} %copy-done.11, f32[320,1024]{1,0:T(8,128)S(1)} %copy-done.10, f32[320,1024]{1,0:T(8,128)S(1)} %copy-done.12), kind=kOutput, calls=%fused_computation.9 | convolution fusion | flops 2354380800 | bytes 18153472 | tf_op jit(solution)/shard_map/dot_general | solution.py:22
  274.3 1.1 all-to-all-done.1
  275.4 1.0 copy-done.1
  276.4 3.6 %all-to-all-start.4 = ((bf16[4,80,3584]{2,1,0:T(8,128)(2,1)}), bf16[4,80,3584]{2,1,0:T(8,128)(2,1)S(1)}, u32[]{:S(2)}, u32[]{:S(2)}) async-start(bf16[4,80,3584]{2,1,0:T(8,128)(2,1)} %bitcast.82), calls=%async_computation.4 | async-start | bytes 4587520 | tf_op jit(solution)/shard_map/all_to_all | solution.py:42
  280.0 4.6 %fusion.25 = bf16[320,1792]{1,0:T(8,128)(2,1)} fusion(bf16[320,1024]{1,0:T(8,128)(2,1)} %copy-done.9, bf16[1,1024,1792]{2,1,0:T(8,128)(2,1)} %all-gather.11.cloned.1.call-done), kind=kOutput, calls=%fused_computation.22 | convolution fusion | flops 1174978560 | bytes 5472256 | tf_op jit(solution)/shard_map/dot_general | solution.py:22
  284.6 22.0 %all-to-all-done.4 = bf16[4,80,3584]{2,1,0:T(8,128)(2,1)S(1)} async-done(((bf16[4,80,3584]{2,1,0:T(8,128)(2,1)}), bf16[4,80,3584]{2,1,0:T(8,128)(2,1)S(1)}, u32[]{:S(2)}, u32[]{:S(2)}) %all-to-all-start.4) | async-done | bytes 2293792 | tf_op jit(solution)/shard_map/all_to_all | solution.py:42
  306.6 4.3 %all-to-all-start.2 = ((bf16[4,80,1792]{2,1,0:T(8,128)(2,1)}), bf16[4,80,1792]{2,1,0:T(8,128)(2,1)}, u32[]{:S(2)}, u32[]{:S(2)}) async-start(bf16[4,80,1792]{2,1,0:T(8,128)(2,1)} %bitcast.83), calls=%async_computation.2 | async-start | bytes 2293760 | tf_op jit(solution)/shard_map/all_to_all | solution.py:42
  310.9 1.9 convolution_convert_fusion.2
  312.8 12.3 %all-to-all-done.2 = bf16[4,80,1792]{2,1,0:T(8,128)(2,1)} async-done(((bf16[4,80,1792]{2,1,0:T(8,128)(2,1)}), bf16[4,80,1792]{2,1,0:T(8,128)(2,1)}, u32[]{:S(2)}, u32[]{:S(2)}) %all-to-all-start.2) | async-done | bytes 1146912 | tf_op jit(solution)/shard_map/all_to_all | solution.py:42
  325.1 3.6 all-to-all-start.5
  328.8 1.1 copy-done.2
  330.4 1.9 fusion.34
  333.8 18.6 %all-to-all-done.5 = bf16[8,448,128]{2,1,0:T(8,128)(2,1)S(1)} async-done(((bf16[8,448,128]{2,1,0:T(8,128)(2,1)}), bf16[8,448,128]{2,1,0:T(8,128)(2,1)S(1)}, u32[]{:S(2)}, u32[]{:S(2)}) %all-to-all-start.5) | async-done | bytes 917536 | tf_op jit(solution)/shard_map/all_to_all | solution.py:82
  352.9 1.3 reshape.70
  (39 shorter events, 5.0 us)
Async XLA Ops:
  7.2 12.0 %copy-start = (bf16[1,128,3584]{2,1,0:T(8,128)(2,1)S(1)}, bf16[1,128,3584]{2,1,0:T(8,128)(2,1)}, u32[]{:S(2)}) copy-start(bf16[1,128,3584]{2,1,0:T(8,128)(2,1)} %param.7) | copy-start | bytes 2752516
  7.2 48.4 %all-gather.11.cloned.1.call-start = ((), (), s32[]{:S(2)}) async-start(), calls=%async_computation.9 | async-start | bytes 4128768 | tf_op jit(solution)/shard_map/all_gather | solution.py:56
  9.4 2.1 copy-start.8
  9.4 2.3 copy-start.3
  9.4 2.3 copy-start.6
  9.5 89.8 %all-gather.9.cloned.1.call-start = ((), (), s32[]{:S(2)}) async-start(), calls=%async_computation.8 | async-start | bytes 4128768 | tf_op jit(solution)/shard_map/all_gather | solution.py:56
  10.2 163.0 %all-gather.5.cloned.1.call-start = ((), (), s32[]{:S(2)}) async-start(), calls=%async_computation.6 | async-start | bytes 8257536 | tf_op jit(solution)/shard_map/all_gather | solution.py:51
  10.9 235.9 %all-gather.7.cloned.1.call-start = ((), (), s32[]{:S(2)}) async-start(), calls=%async_computation.7 | async-start | bytes 8257536 | tf_op jit(solution)/shard_map/all_gather | solution.py:52
  14.0 32.1 %all-to-all-start.3 = ((bf16[4,80,3584]{2,1,0:T(8,128)(2,1)}), bf16[4,80,3584]{2,1,0:T(8,128)(2,1)S(1)}, u32[]{:S(2)}, u32[]{:S(2)}) async-start(bf16[4,80,3584]{2,1,0:T(8,128)(2,1)} %bitcast.17), calls=%async_computation.3 | async-start | bytes 4587520 | tf_op jit(solution)/shard_map/all_to_all | solution.py:42
  46.2 1.5 copy-start.5
  47.6 56.9 %all-to-all-start = ((bf16[4,80,3584]{2,1,0:T(8,128)(2,1)}), bf16[4,80,3584]{2,1,0:T(8,128)(2,1)S(1)}, u32[]{:S(2)}, u32[]{:S(2)}) async-start(bf16[4,80,3584]{2,1,0:T(8,128)(2,1)} %bitcast.5), calls=%async_computation | async-start | bytes 4587520 | tf_op jit(solution)/shard_map/all_to_all | solution.py:42
  246.8 7.2 %copy-start.7 = (bf16[1,1024,1792]{2,1,0:T(8,128)(2,1)S(1)}, bf16[1,1024,1792]{2,1,0:T(8,128)(2,1)}, u32[]{:S(2)}) copy-start(bf16[1,1024,1792]{2,1,0:T(8,128)(2,1)} %all-gather.9.cloned.1.call-done) | copy-start | bytes 11010052
  254.1 2.5 copy-start.9
  256.5 18.9 %all-to-all-start.1 = ((bf16[4,80,1792]{2,1,0:T(8,128)(2,1)}), bf16[4,80,1792]{2,1,0:T(8,128)(2,1)S(1)}, u32[]{:S(2)}, u32[]{:S(2)}) async-start(bf16[4,80,1792]{2,1,0:T(8,128)(2,1)} %bitcast.10), calls=%async_computation.1 | async-start | bytes 2293760 | tf_op jit(solution)/shard_map/all_to_all | solution.py:42
  260.2 6.6 %copy-start.10 = (f32[320,1024]{1,0:T(8,128)S(1)}, f32[320,1024]{1,0:T(8,128)}, u32[]{:S(2)}) copy-start(f32[320,1024]{1,0:T(8,128)} %fusion.28) | copy-start | bytes 3932164
  260.2 6.6 %copy-start.11 = (f32[320,1024]{1,0:T(8,128)S(1)}, f32[320,1024]{1,0:T(8,128)}, u32[]{:S(2)}) copy-start(f32[320,1024]{1,0:T(8,128)} %fusion.6) | copy-start | bytes 3932164
  260.2 6.6 %copy-start.12 = (f32[320,1024]{1,0:T(8,128)S(1)}, f32[320,1024]{1,0:T(8,128)}, u32[]{:S(2)}) copy-start(f32[320,1024]{1,0:T(8,128)} %get-tuple-element.10) | copy-start | bytes 3932164
  275.4 1.0 copy-start.1
  276.4 30.2 %all-to-all-start.4 = ((bf16[4,80,3584]{2,1,0:T(8,128)(2,1)}), bf16[4,80,3584]{2,1,0:T(8,128)(2,1)S(1)}, u32[]{:S(2)}, u32[]{:S(2)}) async-start(bf16[4,80,3584]{2,1,0:T(8,128)(2,1)} %bitcast.82), calls=%async_computation.4 | async-start | bytes 4587520 | tf_op jit(solution)/shard_map/all_to_all | solution.py:42
  306.6 18.5 %all-to-all-start.2 = ((bf16[4,80,1792]{2,1,0:T(8,128)(2,1)}), bf16[4,80,1792]{2,1,0:T(8,128)(2,1)}, u32[]{:S(2)}, u32[]{:S(2)}) async-start(bf16[4,80,1792]{2,1,0:T(8,128)(2,1)} %bitcast.83), calls=%async_computation.2 | async-start | bytes 2293760 | tf_op jit(solution)/shard_map/all_to_all | solution.py:42
  312.8 15.9 %copy-start.4 = (bf16[1,128,3584]{2,1,0:T(8,128)(2,1)S(1)}, bf16[1,128,3584]{2,1,0:T(8,128)(2,1)}, u32[]{:S(2)}) copy-start(bf16[1,128,3584]{2,1,0:T(8,128)(2,1)} %param.8) | copy-start | bytes 2752516
  325.1 27.3 %all-to-all-start.5 = ((bf16[8,448,128]{2,1,0:T(8,128)(2,1)}), bf16[8,448,128]{2,1,0:T(8,128)(2,1)S(1)}, u32[]{:S(2)}, u32[]{:S(2)}) async-start(bf16[8,448,128]{2,1,0:T(8,128)(2,1)} %bitcast.75), calls=%async_computation.5 | async-start | bytes 1835008 | tf_op jit(solution)/shard_map/all_to_all | solution.py:82
  328.6 1.3 copy-start.2
Sparse Core Ops, SparseCore 0:
  10.2 45.2 all-gather.10
  57.8 41.4 all-gather.8
  100.9 72.2 all-gather.4
  174.7 72.0 all-gather.6
where the time goes:
time: 362 us; the launch traced here: 361 us
  waiting for transfers between devices  260 us (72%)
  matrix products  53.6 us (15%)
  starting transfers between devices  24.1 us (7%)
  between operations  14 us (4%)
  local copies, waits for them, and re-layouts  7.67 us (2%)
    all_gather x1, waiting for transfers between devices, local(): gate_matrix = lax.all_gather(w_gate, 'dp', axis=1, tiled=True)[0]  68.7 us
    all_gather x1, waiting for transfers between devices, local(): up_matrix = lax.all_gather(w_up, 'dp', axis=1, tiled=True)[0]  66.9 us
    all_to_all x5, waiting for transfers between devices, over_experts(): lax.all_to_all(rows.reshape(expert_count, capacity, cols), 'expert', spli...  60.3 us
    dot_general x13, matrix products, mm(): return lax.dot_general(a, b, dims, preferred_element_type=F32)  53.6 us
    all_gather x2, waiting for transfers between devices, local(): lax.all_gather(w_down[:, :, s], 'dp', axis=1, tiled=True)[0]  43.2 us
    all_to_all x5, starting transfers between devices, over_experts(): lax.all_to_all(rows.reshape(expert_count, capacity, cols), 'expert', spli...  20.4 us
    all_to_all x1, waiting for transfers between devices, local(): heads = lax.all_to_all(parts, 'dp', split_axis=0, concat_axis=0, tiled=True)  18.6 us
  transfers between devices with their start and end apart: 10, of which 9 were waited for; matrix products, arithmetic and copies ran while one was open for 13% of the time, Pallas kernels for 0%

commit v1 on v0

--- a/solution.py
+++ b/solution.py
@@ -1,3 +1,4 @@
+import functools
 import jax
 import jax.numpy as jnp
 from jax import lax
@@ -6,6 +7,43 @@
 F32 = jnp.float32
 BF16 = jnp.bfloat16
 DOWN_PARTS = 2
+
+
+def use_the_digits(message, ndim_at):
+    found_now = list(message.shape[1:])
+    found_now[ndim_at] *= message.shape[0]
+    return jnp.moveaxis(message, 0, ndim_at).reshape(found_now)
+
+
+def units_connect(inputs, axis_tag, axis_no):
+    lanes = lax.axis_size(axis_tag)
+    arr_now = range(lanes)
+    tall = map(lambda j: (j, (j + 1) % lanes), arr_now)
+    buffer = list(tall)
+    chunks = [(dev_j, h) for h, dev_j in buffer]
+    built, base_arr = ([], [])
+    nth = 0
+    while nth < lanes - 1:
+        if nth % 2 == 0:
+            piece_now = lax.ppermute(
+                built[-1] if built else inputs, axis_name=axis_tag, perm=buffer
+            )
+            built.append(piece_now)
+        else:
+            x_next = lax.ppermute(
+                base_arr[-1] if base_arr else inputs, axis_name=axis_tag, perm=chunks
+            )
+            base_arr.append(x_next)
+        nth = nth + 1
+    res = jnp.stack([*built[::-1], inputs, *base_arr], axis=0)
+    taken_in = lax.axis_index(axis_tag)
+    v_now = len(built)
+    spare = taken_in - v_now
+    res = res[(jnp.arange(lanes) - spare) % lanes]
+    return use_the_digits(res, axis_no)
+
+
+mark_scenes = functools.partial(units_connect, axis_tag="dp", axis_no=1)
 
 
 def placement(route_line, expert_count, capacity):
@@ -53,7 +91,7 @@
     w_down, _ = lax.optimization_barrier((w_down, gate_matrix[:16, :128]))
     step = width // DOWN_PARTS
     spans = [slice(i * step, (i + 1) * step) for i in range(DOWN_PARTS)]
-    downs = [lax.all_gather(w_down[:, :, s], "dp", axis=1, tiled=True)[0] for s in spans]
+    downs = [mark_scenes(w_down[:, :, s])[0] for s in spans]
     routed = over_experts(mm(place, tokens[0]).astype(BF16))
     routed_grad = over_experts(mm(place, scaled_grad).astype(BF16))
     gate_pre = mm(routed, gate_matrix)

time: 362 us -> 324 us (0.90)
  waiting for transfers between devices: 260 us -> 131 us
  starting transfers between devices: 24.1 us -> 92.6 us
  local copies, waits for them, and re-layouts: 7.67 us -> 31.8 us
    ppermute x0 -> x14, starting transfers between devices: none -> 69.7 us  [the longest x6 50.3 us: units_connect(): lax.ppermute(base_arr[-1] if base_arr else inputs, axis_name=axis_tag, pe...]
    all_gather x1, waiting for transfers between devices: 68.7 us -> 0.01 us  [local(): gate_matrix = lax.all_gather(w_gate, 'dp', axis=1, tiled=True)[0]]
    all_gather x1, waiting for transfers between devices: 66.9 us -> 13.8 us  [local(): up_matrix = lax.all_gather(w_up, 'dp', axis=1, tiled=True)[0]]
    ppermute x0 -> x14, waiting for transfers between devices: none -> 49.4 us  [the longest x8 36.2 us: units_connect(): lax.ppermute(built[-1] if built else inputs, axis_name=axis_tag, perm=buf...]
    all_gather x2 -> x0, waiting for transfers between devices: 43.2 us -> none  [local(): lax.all_gather(w_down[:, :, s], 'dp', axis=1, tiled=True)[0]]
    unnamed x26 -> x43, local copies, waits for them, and re-layouts: 3.56 us -> 18 us
    all_to_all x5, waiting for transfers between devices: 60.3 us -> 46.7 us  [over_experts(): lax.all_to_all(rows.reshape(expert_count, capacity, cols), 'expert', spli...]
    gather x0 -> x2, local copies, waits for them, and re-layouts: none -> 9.42 us  [units_connect(): res = res[(jnp.arange(lanes) - spare) % lanes]]
  transfers between devices with their start and end apart: 10 -> 22, of which waited for: 9 -> 12; matrix products, arithmetic and copies ran while one was open for 13% -> 22% of each run, Pallas kernels for 0% -> 0%
where the time goes in v1:
time: 324 us; the launch traced here: 323 us
  waiting for transfers between devices  131 us (40%)
  starting transfers between devices  92.6 us (29%)
  matrix products  50 us (15%)
  local copies, waits for them, and re-layouts  31.8 us (10%)
  between operations  14.3 us (4%)
    ppermute x6, starting transfers between devices, units_connect(): lax.ppermute(base_arr[-1] if base_arr else inputs, axis_name=axis_tag, pe...  50.3 us
    dot_general x13, matrix products, mm(): return lax.dot_general(a, b, dims, preferred_element_type=F32)  50 us
    all_to_all x5, waiting for transfers between devices, over_experts(): lax.all_to_all(rows.reshape(expert_count, capacity, cols), 'expert', spli...  46.7 us
    ppermute x8, waiting for transfers between devices, units_connect(): lax.ppermute(built[-1] if built else inputs, axis_name=axis_tag, perm=buf...  36.2 us
    all_to_all x1, waiting for transfers between devices, local(): heads = lax.all_to_all(parts, 'dp', split_axis=0, concat_axis=0, tiled=True)  19.8 us
    ppermute x8, starting transfers between devices, units_connect(): lax.ppermute(built[-1] if built else inputs, axis_name=axis_tag, perm=buf...  19.3 us
    all_to_all x5, starting transfers between devices, over_experts(): lax.all_to_all(rows.reshape(expert_count, capacity, cols), 'expert', spli...  19.1 us
    unnamed x43, local copies, waits for them, and re-layouts  18 us
  transfers between devices with their start and end apart: 22, of which 12 were waited for; matrix products, arithmetic and copies ran while one was open for 22% of the time, Pallas kernels for 0%

profile of v1, /device:TPU:0, one launch (start us, length us, event | category | flops | bytes accessed | tf_op | source)
XLA Modules:
  0.0 322.8 jit_solution(11730055464584579009)
XLA Ops:
  10.0 2.7 collective-permute-start.7
  12.7 7.7 %collective-permute-done = bf16[1,128,1792]{2,1,0:T(8,128)(2,1)S(1)} collective-permute-done((bf16[1,128,1792]{2,1,0:T(8,128)(2,1)}, bf16[1,128,1792]{2,1,0:T(8,128)(2,1)S(1)}, u32[]{:S(2)}, u32[]{:S(2)}) %collective-permute-start) | collective-permute-done | bytes 458784 | tf_op jit(solution)/shard_map/ppermute | solution.py:28
  20.4 3.5 %collective-permute-start.4 = (bf16[1,128,1792]{2,1,0:T(8,128)(2,1)}, bf16[1,128,1792]{2,1,0:T(8,128)(2,1)}, u32[]{:S(2)}, u32[]{:S(2)}) collective-permute-start(bf16[1,128,1792]{2,1,0:T(8,128)(2,1)} %get-tuple-element.9), channel_id=1, source_target_pairs={{4,0},{8,4},{12,8},{16,12},{20,16},{24,20},{28,24},{0,28},{5,1},{9... | collective-permute-start | bytes 1376264 | tf_op jit(solution)/shard_map/ppermute | solution.py:33
  27.7 17.6 %collective-permute-done.1 = bf16[1,128,1792]{2,1,0:T(8,128)(2,1)} collective-permute-done((bf16[1,128,1792]{2,1,0:T(8,128)(2,1)S(1)}, bf16[1,128,1792]{2,1,0:T(8,128)(2,1)}, u32[]{:S(2)}, u32[]{:S(2)}) %collective-permute-start.1) | collective-permute-done | bytes 458784 | tf_op jit(solution)/shard_map/ppermute | solution.py:28
  49.6 4.5 %all-to-all-start.3 = ((bf16[4,80,3584]{2,1,0:T(8,128)(2,1)}), bf16[4,80,3584]{2,1,0:T(8,128)(2,1)}, u32[]{:S(2)}, u32[]{:S(2)}) async-start(bf16[4,80,3584]{2,1,0:T(8,128)(2,1)} %bitcast.36), calls=%async_computation.3 | async-start | bytes 4587520 | tf_op jit(solution)/shard_map/all_to_all | solution.py:80
  54.1 2.6 collective-permute-start.5
  56.7 7.8 %collective-permute-done.11 = bf16[1,128,1792]{2,1,0:T(8,128)(2,1)} collective-permute-done((bf16[1,128,1792]{2,1,0:T(8,128)(2,1)S(1)}, bf16[1,128,1792]{2,1,0:T(8,128)(2,1)}, u32[]{:S(2)}, u32[]{:S(2)}) %collective-permute-start.11) | collective-permute-done | bytes 458784 | tf_op jit(solution)/shard_map/ppermute | solution.py:33
  64.5 15.8 %collective-permute-start.12 = (bf16[1,128,1792]{2,1,0:T(8,128)(2,1)}, bf16[1,128,1792]{2,1,0:T(8,128)(2,1)S(1)}, u32[]{:S(2)}, u32[]{:S(2)}) collective-permute-start(bf16[1,128,1792]{2,1,0:T(8,128)(2,1)} %collective-permute-done.11), channel_id=1, source_target_pairs={{4,0},{8,4},{12,8},{16,12},{20,16},{24,20},{28,24},{0,28},{5,1},{9... | collective-permute-start | bytes 1376264 | tf_op jit(solution)/shard_map/ppermute | solution.py:33
  80.3 10.3 %collective-permute-start.9 = (bf16[1,128,1792]{2,1,0:T(8,128)(2,1)}, bf16[1,128,1792]{2,1,0:T(8,128)(2,1)S(1)}, u32[]{:S(2)}, u32[]{:S(2)}) collective-permute-start(bf16[1,128,1792]{2,1,0:T(8,128)(2,1)} %collective-permute-done.8), channel_id=1, source_target_pairs={{0,4},{4,8},{8,12},{12,16},{16,20},{20,24},{24,28},{28,0},{1,5},{5... | collective-permute-start | bytes 1376264 | tf_op jit(solution)/shard_map/ppermute | solution.py:28
  96.5 5.4 %collective-permute-done.12 = bf16[1,128,1792]{2,1,0:T(8,128)(2,1)S(1)} collective-permute-done((bf16[1,128,1792]{2,1,0:T(8,128)(2,1)}, bf16[1,128,1792]{2,1,0:T(8,128)(2,1)S(1)}, u32[]{:S(2)}, u32[]{:S(2)}) %collective-permute-start.12) | collective-permute-done | bytes 458784 | tf_op jit(solution)/shard_map/ppermute | solution.py:33
  101.8 26.6 %collective-permute-start.13 = (bf16[1,128,1792]{2,1,0:T(8,128)(2,1)S(1)}, bf16[1,128,1792]{2,1,0:T(8,128)(2,1)S(1)}, u32[]{:S(2)}, u32[]{:S(2)}) collective-permute-start(bf16[1,128,1792]{2,1,0:T(8,128)(2,1)S(1)} %collective-permute-done.12), channel_id=1, source_target_pairs={{4,0},{8,4},{12,8},{16,12},{20,16},{24,20},{28,24},{0,28},{5,1},{9... | collective-permute-start | bytes 1376264 | tf_op jit(solution)/shard_map/ppermute | solution.py:33
  133.7 9.4 %collective-permute-done.10 = bf16[1,128,1792]{2,1,0:T(8,128)(2,1)S(1)} collective-permute-done((bf16[1,128,1792]{2,1,0:T(8,128)(2,1)S(1)}, bf16[1,128,1792]{2,1,0:T(8,128)(2,1)S(1)}, u32[]{:S(2)}, u32[]{:S(2)}) %collective-permute-start.10) | collective-permute-done | bytes 458784 | tf_op jit(solution)/shard_map/ppermute | solution.py:28
  152.9 4.7 %gather_fusion = bf16[8,128,1792]{2,1,0:T(8,128)(2,1)} fusion(bf16[8,128,1792]{2,1,0:T(8,128)(2,1)} %bitcast.17, s32[1024]{0:T(1024)S(1)} %pad_clamp_fusion), kind=kCustom, calls=%fused_computation | custom fusion | bytes 7340064 | tf_op jit(solution)/shard_map/gather | solution.py:42
  159.5 3.8 %all-to-all-start = ((bf16[4,80,3584]{2,1,0:T(8,128)(2,1)}), bf16[4,80,3584]{2,1,0:T(8,128)(2,1)S(1)}, u32[]{:S(2)}, u32[]{:S(2)}) async-start(bf16[4,80,3584]{2,1,0:T(8,128)(2,1)} %bitcast.5), calls=%async_computation | async-start | bytes 4587520 | tf_op jit(solution)/shard_map/all_to_all | solution.py:80
  165.0 4.7 %gather_fusion.1 = bf16[8,128,1792]{2,1,0:T(8,128)(2,1)} fusion(bf16[8,128,1792]{2,1,0:T(8,128)(2,1)} %bitcast.30, s32[1024]{0:T(1024)S(1)} %pad_clamp_fusion), kind=kCustom, calls=%fused_computation.1 | custom fusion | bytes 7340064 | tf_op jit(solution)/shard_map/gather | solution.py:42
  169.7 4.0 %fusion.16 = f32[320,1024]{1,0:T(8,128)S(1)} fusion(bf16[1024,1792]{1,0:T(8,128)(2,1)} %bitcast.106, bf16[320,3584]{1,0:T(8,128)(2,1)} %bitcast.37), kind=kOutput, calls=%fused_computation.25 | convolution fusion | flops 1174405120 | bytes 6127616 | tf_op jit(solution)/shard_map/dot_general | solution.py:60
  173.7 3.8 %convolution_add_fusion = f32[320,1024]{1,0:T(8,128)} fusion(f32[320,1024]{1,0:T(8,128)S(1)} %fusion.16, bf16[1024,1792]{1,0:T(8,128)(2,1)S(1)} %bitcast.105, bf16[320,3584]{1,0:T(8,128)(2,1)} %bitcast.37), kind=kOutput, calls=%fused_computation.18 | convolution fusion | flops 1174732800 | bytes 7438336 | tf_op jit(solution)/shard_map/dot_general | solution.py:60
  177.5 11.2 %all-to-all-done = bf16[4,80,3584]{2,1,0:T(8,128)(2,1)S(1)} async-done(((bf16[4,80,3584]{2,1,0:T(8,128)(2,1)}), bf16[4,80,3584]{2,1,0:T(8,128)(2,1)S(1)}, u32[]{:S(2)}, u32[]{:S(2)}) %all-to-all-start) | async-done | bytes 2293792 | tf_op jit(solution)/shard_map/all_to_all | solution.py:80
  188.7 6.8 %fusion.6 = f32[320,1024]{1,0:T(8,128)} fusion(bf16[320,3584]{1,0:T(8,128)(2,1)S(1)} %bitcast.108, bf16[1,3584,1024]{2,1,0:T(8,128)(2,1)} %all-gather.3.cloned.1.call-done), kind=kOutput, calls=%fused_computation.8 | convolution fusion | flops 2348810240 | bytes 10944512 | tf_op jit(solution)/shard_map/dot_general | solution.py:60
  195.5 13.8 %all-gather.5.cloned.1.call-done = bf16[1,3584,1024]{2,1,0:T(8,128)(2,1)} async-done(((bf16[1,448,1024]{2,1,0:T(8,128)(2,1)}), bf16[1,3584,1024]{2,1,0:T(8,128)(2,1)}) %all-gather.5.cloned.1.call-update) | async-done | bytes 7340048 | tf_op jit(solution)/shard_map/all_gather | solution.py:90
  209.3 7.3 %multiply_convert_fusion.3 = (bf16[320,1024]{1,0:T(8,128)(2,1)S(1)}, f32[320,1024]{1,0:T(8,128)}) fusion(f32[320,1024]{1,0:T(8,128)} %fusion.6, bf16[320,3584]{1,0:T(8,128)(2,1)S(1)} %bitcast.109, bf16[1,3584,1024]{2,1,0:T(8,128)(2,1)} %all-gather.5.cloned.1.call-done), kind=kOutput, calls=%fused_computation.21 | convolution fusion | flops 2350776320 | bytes 12910592 | tf_op jit(solution)/shard_map/dot_general | solution.py:60
  216.6 2.4 convolution_convert_fusion.4
  219.0 3.7 %all-to-all-start.1 = ((bf16[4,80,1792]{2,1,0:T(8,128)(2,1)}), bf16[4,80,1792]{2,1,0:T(8,128)(2,1)S(1)}, u32[]{:S(2)}, u32[]{:S(2)}) async-start(bf16[4,80,1792]{2,1,0:T(8,128)(2,1)} %bitcast.20), calls=%async_computation.1 | async-start | bytes 2293760 | tf_op jit(solution)/shard_map/all_to_all | solution.py:80
  222.7 6.6 %fusion = f32[320,3584]{1,0:T(8,128)S(1)} fusion(bf16[1,3584,1024]{2,1,0:T(8,128)(2,1)} %all-gather.5.cloned.1.call-done, f32[320,1024]{1,0:T(8,128)} %convolution_add_fusion, f32[320,1024]{1,0:T(8,128)} %fusion.6), kind=kOutput, calls=%fused_computation.2 | convolution fusion | flops 2350776320 | bytes 14548992 | tf_op jit(solution)/shard_map/dot_general | solution.py:60
  229.3 7.4 %fusion.11 = bf16[320,3584]{1,0:T(8,128)(2,1)} fusion(f32[320,3584]{1,0:T(8,128)S(1)} %fusion, bf16[1,3584,1024]{2,1,0:T(8,128)(2,1)} %all-gather.3.cloned.1.call-done, f32[320,1024]{1,0:T(8,128)S(1)} %copy-done.13, f32[320,1024]{1,0:T(8,128)S(1)} %copy-done.12, f32[320,1024]{1,0:T(8,128)S(1)} %copy-done.14), kind=kOutput, calls=%fused_computation.11 | convolution fusion | flops 2354380800 | bytes 18153472 | tf_op jit(solution)/shard_map/dot_general | solution.py:60
  238.8 3.6 %all-to-all-start.4 = ((bf16[4,80,3584]{2,1,0:T(8,128)(2,1)}), bf16[4,80,3584]{2,1,0:T(8,128)(2,1)S(1)}, u32[]{:S(2)}, u32[]{:S(2)}) async-start(bf16[4,80,3584]{2,1,0:T(8,128)(2,1)} %bitcast.110), calls=%async_computation.4 | async-start | bytes 4587520 | tf_op jit(solution)/shard_map/all_to_all | solution.py:80
  242.5 4.4 %convolution_convert_fusion.3 = bf16[320,1792]{1,0:T(8,128)(2,1)} fusion(bf16[320,1024]{1,0:T(8,128)(2,1)S(1)} %get-tuple-element.11, bf16[1024,1792]{1,0:T(8,128)(2,1)} %bitcast.104), kind=kOutput, calls=%fused_computation.15 | convolution fusion | flops 1174978560 | bytes 5472256 | tf_op jit(solution)/shard_map/dot_general | solution.py:60
  246.9 22.2 %all-to-all-done.4 = bf16[4,80,3584]{2,1,0:T(8,128)(2,1)S(1)} async-done(((bf16[4,80,3584]{2,1,0:T(8,128)(2,1)}), bf16[4,80,3584]{2,1,0:T(8,128)(2,1)S(1)}, u32[]{:S(2)}, u32[]{:S(2)}) %all-to-all-start.4) | async-done | bytes 2293792 | tf_op jit(solution)/shard_map/all_to_all | solution.py:80
  269.1 3.5 %all-to-all-start.2 = ((bf16[4,80,1792]{2,1,0:T(8,128)(2,1)}), bf16[4,80,1792]{2,1,0:T(8,128)(2,1)S(1)}, u32[]{:S(2)}, u32[]{:S(2)}) async-start(bf16[4,80,1792]{2,1,0:T(8,128)(2,1)} %bitcast.111), calls=%async_computation.2 | async-start | bytes 2293760 | tf_op jit(solution)/shard_map/all_to_all | solution.py:80
  274.5 12.2 %all-to-all-done.2 = bf16[4,80,1792]{2,1,0:T(8,128)(2,1)S(1)} async-done(((bf16[4,80,1792]{2,1,0:T(8,128)(2,1)}), bf16[4,80,1792]{2,1,0:T(8,128)(2,1)S(1)}, u32[]{:S(2)}, u32[]{:S(2)}) %all-to-all-start.2) | async-done | bytes 1146912 | tf_op jit(solution)/shard_map/all_to_all | solution.py:80
  286.7 3.7 %all-to-all-start.5 = ((bf16[8,448,128]{2,1,0:T(8,128)(2,1)}), bf16[8,448,128]{2,1,0:T(8,128)(2,1)S(1)}, u32[]{:S(2)}, u32[]{:S(2)}) async-start(bf16[8,448,128]{2,1,0:T(8,128)(2,1)} %bitcast.40), calls=%async_computation.5 | async-start | bytes 1835008 | tf_op jit(solution)/shard_map/all_to_all | solution.py:120
  294.3 19.8 %all-to-all-done.5 = bf16[8,448,128]{2,1,0:T(8,128)(2,1)S(1)} async-done(((bf16[8,448,128]{2,1,0:T(8,128)(2,1)}), bf16[8,448,128]{2,1,0:T(8,128)(2,1)S(1)}, u32[]{:S(2)}, u32[]{:S(2)}) %all-to-all-start.5) | async-done | bytes 917536 | tf_op jit(solution)/shard_map/all_to_all | solution.py:120
  (84 shorter events, 45.1 us)
Async XLA Ops:
  7.2 85.3 %copy-start = (bf16[1,128,3584]{2,1,0:T(8,128)(2,1)S(1)}, bf16[1,128,3584]{2,1,0:T(8,128)(2,1)}, u32[]{:S(2)}) copy-start(bf16[1,128,3584]{2,1,0:T(8,128)(2,1)} %param.7) | copy-start | bytes 2752516
  7.2 16.8 %copy-start.11 = (s32[1,128]{1,0:T(1,128)S(1)}, s32[1,128]{1,0:T(1,128)}, u32[]{:S(2)}) copy-start(s32[1,128]{1,0:T(1,128)} %param.9) | copy-start | bytes 1540
  7.2 40.2 %copy-start.10 = (f32[1,128]{1,0:T(1,128)S(1)}, f32[1,128]{1,0:T(1,128)}, u32[]{:S(2)}) copy-start(f32[1,128]{1,0:T(1,128)} %param.10) | copy-start | bytes 1540
  7.2 40.2 %copy-start.7 = (bf16[1,128,3584]{2,1,0:T(8,128)(2,1)S(1)}, bf16[1,128,3584]{2,1,0:T(8,128)(2,1)}, u32[]{:S(2)}) copy-start(bf16[1,128,3584]{2,1,0:T(8,128)(2,1)} %param.8) | copy-start | bytes 2752516
  7.2 181.4 %all-gather.3.cloned.1.call-start = ((), (), s32[]{:S(2)}) async-start(), calls=%async_computation.6 | async-start | bytes 8257536 | tf_op jit(solution)/shard_map/all_gather | solution.py:89
  8.0 201.3 %all-gather.5.cloned.1.call-start = ((), (), s32[]{:S(2)}) async-start(), calls=%async_computation.7 | async-start | bytes 8257536 | tf_op jit(solution)/shard_map/all_gather | solution.py:90
  9.5 10.9 %collective-permute-start = (bf16[1,128,1792]{2,1,0:T(8,128)(2,1)}, bf16[1,128,1792]{2,1,0:T(8,128)(2,1)S(1)}, u32[]{:S(2)}, u32[]{:S(2)}) collective-permute-start(bf16[1,128,1792]{2,1,0:T(8,128)(2,1)} %get-tuple-element.9), channel_id=1, source_target_pairs={{0,4},{4,8},{8,12},{12,16},{16,20},{20,24},{24,28},{28,0},{1,5},{5... | collective-permute-start | bytes 1376264 | tf_op jit(solution)/shard_map/ppermute | solution.py:28
  10.0 15.7 %collective-permute-start.7 = (bf16[1,128,1792]{2,1,0:T(8,128)(2,1)S(1)}, bf16[1,128,1792]{2,1,0:T(8,128)(2,1)}, u32[]{:S(2)}, u32[]{:S(2)}) collective-permute-start(bf16[1,128,1792]{2,1,0:T(8,128)(2,1)S(1)} %get-tuple-element.10), channel_id=1, source_target_pairs={{0,4},{4,8},{8,12},{12,16},{16,20},{20,24},{24,28},{28,0},{1,5},{5... | collective-permute-start | bytes 1376264 | tf_op jit(solution)/shard_map/ppermute | solution.py:28
  20.4 24.9 %collective-permute-start.1 = (bf16[1,128,1792]{2,1,0:T(8,128)(2,1)S(1)}, bf16[1,128,1792]{2,1,0:T(8,128)(2,1)}, u32[]{:S(2)}, u32[]{:S(2)}) collective-permute-start(bf16[1,128,1792]{2,1,0:T(8,128)(2,1)S(1)} %collective-permute-done), channel_id=1, source_target_pairs={{0,4},{4,8},{8,12},{12,16},{16,20},{20,24},{24,28},{28,0},{1,5},{5... | collective-permute-start | bytes 1376264 | tf_op jit(solution)/shard_map/ppermute | solution.py:28
  20.4 33.7 %collective-permute-start.4 = (bf16[1,128,1792]{2,1,0:T(8,128)(2,1)}, bf16[1,128,1792]{2,1,0:T(8,128)(2,1)}, u32[]{:S(2)}, u32[]{:S(2)}) collective-permute-start(bf16[1,128,1792]{2,1,0:T(8,128)(2,1)} %get-tuple-element.9), channel_id=1, source_target_pairs={{4,0},{8,4},{12,8},{16,12},{20,16},{24,20},{28,24},{0,28},{5,1},{9... | collective-permute-start | bytes 1376264 | tf_op jit(solution)/shard_map/ppermute | solution.py:33
  24.0 40.6 %collective-permute-start.11 = (bf16[1,128,1792]{2,1,0:T(8,128)(2,1)S(1)}, bf16[1,128,1792]{2,1,0:T(8,128)(2,1)}, u32[]{:S(2)}, u32[]{:S(2)}) collective-permute-start(bf16[1,128,1792]{2,1,0:T(8,128)(2,1)S(1)} %get-tuple-element.10), channel_id=1, source_target_pairs={{4,0},{8,4},{12,8},{16,12},{20,16},{24,20},{28,24},{0,28},{5,1},{9... | collective-permute-start | bytes 1376264 | tf_op jit(solution)/shard_map/ppermute | solution.py:33
  25.7 54.6 %collective-permute-start.8 = (bf16[1,128,1792]{2,1,0:T(8,128)(2,1)}, bf16[1,128,1792]{2,1,0:T(8,128)(2,1)}, u32[]{:S(2)}, u32[]{:S(2)}) collective-permute-start(bf16[1,128,1792]{2,1,0:T(8,128)(2,1)} %collective-permute-done.7), channel_id=1, source_target_pairs={{0,4},{4,8},{8,12},{12,16},{16,20},{20,24},{24,28},{28,0},{1,5},{5... | collective-permute-start | bytes 1376264 | tf_op jit(solution)/shard_map/ppermute | solution.py:28
  45.3 45.3 %collective-permute-start.2 = (bf16[1,128,1792]{2,1,0:T(8,128)(2,1)}, bf16[1,128,1792]{2,1,0:T(8,128)(2,1)}, u32[]{:S(2)}, u32[]{:S(2)}) collective-permute-start(bf16[1,128,1792]{2,1,0:T(8,128)(2,1)} %collective-permute-done.1), channel_id=1, source_target_pairs={{0,4},{4,8},{8,12},{12,16},{16,20},{20,24},{24,28},{28,0},{1,5},{5... | collective-permute-start | bytes 1376264 | tf_op jit(solution)/shard_map/ppermute | solution.py:28
  49.6 109.9 %all-to-all-start.3 = ((bf16[4,80,3584]{2,1,0:T(8,128)(2,1)}), bf16[4,80,3584]{2,1,0:T(8,128)(2,1)}, u32[]{:S(2)}, u32[]{:S(2)}) async-start(bf16[4,80,3584]{2,1,0:T(8,128)(2,1)} %bitcast.36), calls=%async_computation.3 | async-start | bytes 4587520 | tf_op jit(solution)/shard_map/all_to_all | solution.py:80
  54.1 40.5 %collective-permute-start.5 = (bf16[1,128,1792]{2,1,0:T(8,128)(2,1)}, bf16[1,128,1792]{2,1,0:T(8,128)(2,1)S(1)}, u32[]{:S(2)}, u32[]{:S(2)}) collective-permute-start(bf16[1,128,1792]{2,1,0:T(8,128)(2,1)} %collective-permute-done.4), channel_id=1, source_target_pairs={{4,0},{8,4},{12,8},{16,12},{20,16},{24,20},{28,24},{0,28},{5,1},{9... | collective-permute-start | bytes 1376264 | tf_op jit(solution)/shard_map/ppermute | solution.py:33
  64.5 37.3 %collective-permute-start.12 = (bf16[1,128,1792]{2,1,0:T(8,128)(2,1)}, bf16[1,128,1792]{2,1,0:T(8,128)(2,1)S(1)}, u32[]{:S(2)}, u32[]{:S(2)}) collective-permute-start(bf16[1,128,1792]{2,1,0:T(8,128)(2,1)} %collective-permute-done.11), channel_id=1, source_target_pairs={{4,0},{8,4},{12,8},{16,12},{20,16},{24,20},{28,24},{0,28},{5,1},{9... | collective-permute-start | bytes 1376264 | tf_op jit(solution)/shard_map/ppermute | solution.py:33
  80.3 48.1 %collective-permute-start.9 = (bf16[1,128,1792]{2,1,0:T(8,128)(2,1)}, bf16[1,128,1792]{2,1,0:T(8,128)(2,1)S(1)}, u32[]{:S(2)}, u32[]{:S(2)}) collective-permute-start(bf16[1,128,1792]{2,1,0:T(8,128)(2,1)} %collective-permute-done.8), channel_id=1, source_target_pairs={{0,4},{4,8},{8,12},{12,16},{16,20},{20,24},{24,28},{28,0},{1,5},{5... | collective-permute-start | bytes 1376264 | tf_op jit(solution)/shard_map/ppermute | solution.py:28
  90.7 37.8 %collective-permute-start.3 = (bf16[1,128,1792]{2,1,0:T(8,128)(2,1)}, bf16[1,128,1792]{2,1,0:T(8,128)(2,1)S(1)}, u32[]{:S(2)}, u32[]{:S(2)}) collective-permute-start(bf16[1,128,1792]{2,1,0:T(8,128)(2,1)} %collective-permute-done.2), channel_id=1, source_target_pairs={{0,4},{4,8},{8,12},{12,16},{16,20},{20,24},{24,28},{28,0},{1,5},{5... | collective-permute-start | bytes 1376264 | tf_op jit(solution)/shard_map/ppermute | solution.py:28
  94.7 38.2 %copy-start.9 = (bf16[1,128,1792]{2,1,0:T(8,128)(2,1)S(1)}, bf16[1,128,1792]{2,1,0:T(8,128)(2,1)}, u32[]{:S(2)}) copy-start(bf16[1,128,1792]{2,1,0:T(8,128)(2,1)} %copy-done.8) | copy-start | bytes 1376260
  94.7 57.5 %collective-permute-start.6 = (bf16[1,128,1792]{2,1,0:T(8,128)(2,1)S(1)}, bf16[1,128,1792]{2,1,0:T(8,128)(2,1)S(1)}, u32[]{:S(2)}, u32[]{:S(2)}) collective-permute-start(bf16[1,128,1792]{2,1,0:T(8,128)(2,1)S(1)} %collective-permute-done.5), channel_id=1, source_target_pairs={{4,0},{8,4},{12,8},{16,12},{20,16},{24,20},{28,24},{0,28},{5,1},{9... | collective-permute-start | bytes 1376264 | tf_op jit(solution)/shard_map/ppermute | solution.py:33
  101.8 62.3 %collective-permute-start.13 = (bf16[1,128,1792]{2,1,0:T(8,128)(2,1)S(1)}, bf16[1,128,1792]{2,1,0:T(8,128)(2,1)S(1)}, u32[]{:S(2)}, u32[]{:S(2)}) collective-permute-start(bf16[1,128,1792]{2,1,0:T(8,128)(2,1)S(1)} %collective-permute-done.12), channel_id=1, source_target_pairs={{4,0},{8,4},{12,8},{16,12},{20,16},{24,20},{28,24},{0,28},{5,1},{9... | collective-permute-start | bytes 1376264 | tf_op jit(solution)/shard_map/ppermute | solution.py:33
  128.4 14.7 %collective-permute-start.10 = (bf16[1,128,1792]{2,1,0:T(8,128)(2,1)S(1)}, bf16[1,128,1792]{2,1,0:T(8,128)(2,1)S(1)}, u32[]{:S(2)}, u32[]{:S(2)}) collective-permute-start(bf16[1,128,1792]{2,1,0:T(8,128)(2,1)S(1)} %collective-permute-done.9), channel_id=1, source_target_pairs={{0,4},{4,8},{8,12},{12,16},{16,20},{20,24},{24,28},{28,0},{1,5},{5... | collective-permute-start | bytes 1376264 | tf_op jit(solution)/shard_map/ppermute | solution.py:28
  159.5 29.1 %all-to-all-start = ((bf16[4,80,3584]{2,1,0:T(8,128)(2,1)}), bf16[4,80,3584]{2,1,0:T(8,128)(2,1)S(1)}, u32[]{:S(2)}, u32[]{:S(2)}) async-start(bf16[4,80,3584]{2,1,0:T(8,128)(2,1)} %bitcast.5), calls=%async_computation | async-start | bytes 4587520 | tf_op jit(solution)/shard_map/all_to_all | solution.py:80
  209.3 7.3 %copy-start.6 = (bf16[8,128,1792]{2,1,0:T(8,128)(2,1)S(1)}, bf16[8,128,1792]{2,1,0:T(8,128)(2,1)}, u32[]{:S(2)}) copy-start(bf16[8,128,1792]{2,1,0:T(8,128)(2,1)} %gather_fusion) | copy-start | bytes 11010052
  219.0 18.9 %all-to-all-start.1 = ((bf16[4,80,1792]{2,1,0:T(8,128)(2,1)}), bf16[4,80,1792]{2,1,0:T(8,128)(2,1)S(1)}, u32[]{:S(2)}, u32[]{:S(2)}) async-start(bf16[4,80,1792]{2,1,0:T(8,128)(2,1)} %bitcast.20), calls=%async_computation.1 | async-start | bytes 2293760 | tf_op jit(solution)/shard_map/all_to_all | solution.py:80
  222.7 6.6 %copy-start.12 = (f32[320,1024]{1,0:T(8,128)S(1)}, f32[320,1024]{1,0:T(8,128)}, u32[]{:S(2)}) copy-start(f32[320,1024]{1,0:T(8,128)} %convolution_add_fusion) | copy-start | bytes 3932164
  222.7 6.6 %copy-start.13 = (f32[320,1024]{1,0:T(8,128)S(1)}, f32[320,1024]{1,0:T(8,128)}, u32[]{:S(2)}) copy-start(f32[320,1024]{1,0:T(8,128)} %fusion.6) | copy-start | bytes 3932164
  222.7 6.6 %copy-start.14 = (f32[320,1024]{1,0:T(8,128)S(1)}, f32[320,1024]{1,0:T(8,128)}, u32[]{:S(2)}) copy-start(f32[320,1024]{1,0:T(8,128)} %get-tuple-element.12) | copy-start | bytes 3932164
  238.8 30.2 %all-to-all-start.4 = ((bf16[4,80,3584]{2,1,0:T(8,128)(2,1)}), bf16[4,80,3584]{2,1,0:T(8,128)(2,1)S(1)}, u32[]{:S(2)}, u32[]{:S(2)}) async-start(bf16[4,80,3584]{2,1,0:T(8,128)(2,1)} %bitcast.110), calls=%async_computation.4 | async-start | bytes 4587520 | tf_op jit(solution)/shard_map/all_to_all | solution.py:80
  269.1 17.6 %all-to-all-start.2 = ((bf16[4,80,1792]{2,1,0:T(8,128)(2,1)}), bf16[4,80,1792]{2,1,0:T(8,128)(2,1)S(1)}, u32[]{:S(2)}, u32[]{:S(2)}) async-start(bf16[4,80,1792]{2,1,0:T(8,128)(2,1)} %bitcast.111), calls=%async_computation.2 | async-start | bytes 2293760 | tf_op jit(solution)/shard_map/all_to_all | solution.py:80
  286.7 27.4 %all-to-all-start.5 = ((bf16[8,448,128]{2,1,0:T(8,128)(2,1)}), bf16[8,448,128]{2,1,0:T(8,128)(2,1)S(1)}, u32[]{:S(2)}, u32[]{:S(2)}) async-start(bf16[8,448,128]{2,1,0:T(8,128)(2,1)} %bitcast.40), calls=%async_computation.5 | async-start | bytes 1835008 | tf_op jit(solution)/shard_map/all_to_all | solution.py:120
  293.3 22.7 %copy-start.1 = (bf16[1,128,3584]{2,1,0:T(8,128)(2,1)S(1)}, bf16[1,128,3584]{2,1,0:T(8,128)(2,1)}, u32[]{:S(2)}) copy-start(bf16[1,128,3584]{2,1,0:T(8,128)(2,1)} %param.7) | copy-start | bytes 2752516
  (5 other events, 16.9 us)
Sparse Core Ops, SparseCore 0:
  9.7 123.0 all-gather.2
  134.5 74.7 all-gather.4
